TPU v7x, 32 devices: a whole 2x2x4 slice. The times are simulated.
32 devices in a mesh: vol: 2 (over y), space: 16 (over z, x, core).
Axes of the slice: x: 2, y: 2, z: 4, core: 2. Of those that a mesh axis runs over, the one named last changes fastest.
Arguments:
- volume: bfloat16 [2, 32, 64, 8, 128], P('vol', None, 'space'), may hold values from -80 to 80
- conv_weight: bfloat16 [32, 32, 3, 3, 3], replicated, may hold values from -0.21875 to 0.21875
- conv_bias: float32 [32], replicated, may hold values from -3 to 3
- basis: float32 [864, 864], replicated, may hold values from -3 to 3
- damping: float32 [1], replicated, may hold values from 0.5 to 2
Outputs:
- projected: float32 [864, 864], P('vol')
All inputs are finite; a program needn't handle non-finite values.
Results may differ from a plain program's by a relative error of at most 0.0019.
Values may be sent and summed in bfloat16 or wider, within the bound.
A program may use at most 64 MiB of HBM per device.

v0:
```python
import jax
import jax.numpy as jnp
from jax import lax
from jax.sharding import PartitionSpec as P


def shifted(block, axis, distance):
    devices = range(lax.axis_size(axis))
    route = [(i - distance, i) for i in devices if i - distance in devices]
    return lax.ppermute(block, axis, route)


def extract_patches(activated):
    chans, planes, rows_y, cols_z = activated.shape
    viewed = activated.reshape(chans, planes // 4, 4, rows_y // 4, 4, cols_z // 4, 4)[
        :, :, 1:, :, 1:, :, 1:
    ]
    viewed = viewed.transpose(0, 2, 4, 6, 1, 3, 5)
    return viewed.reshape(chans * 27, -1)


def body(volume, conv_weight, conv_bias, basis, damping):
    local_block = volume[0]
    from_above = shifted(local_block[:, 0:1], "space", -1)
    zero_plane = jnp.zeros_like(from_above)
    stacked = jnp.concatenate([zero_plane, local_block, from_above], axis=1)
    conv_out = lax.conv_general_dilated(
        stacked[None],
        conv_weight,
        (1, 1, 1),
        [(0, 0), (1, 1), (1, 1)],
        dimension_numbers=("NCDHW", "OIDHW", "NCDHW"),
        preferred_element_type=jnp.float32,
    )[0]
    activated = jnp.maximum(conv_out + conv_bias[:, None, None, None], 0.0).astype(jnp.bfloat16)
    patch_cols = extract_patches(activated)
    local_gram = jnp.dot(patch_cols, patch_cols.T, preferred_element_type=jnp.float32)
    gram_width = local_gram.shape[0]
    total_patches = patch_cols.shape[1] * lax.axis_size("space") * lax.axis_size("vol")
    panel_rows = gram_width // lax.axis_size("vol")
    row_start = lax.axis_index("vol") * panel_rows
    partial_rows = lax.psum_scatter(
        local_gram.astype(jnp.bfloat16), "vol", scatter_dimension=0, tiled=True
    ).astype(jnp.float32)
    row_panel = lax.psum(partial_rows, "space")
    diag_block = lax.dynamic_slice_in_dim(row_panel, row_start, panel_rows, 1)
    trace_value = lax.psum(jnp.trace(diag_block), "vol")
    normed_panel = row_panel / total_patches
    mean_diagonal = trace_value / total_patches / gram_width
    basis_rows = lax.dynamic_slice_in_dim(basis, row_start, panel_rows, 0)
    product = jnp.dot(
        normed_panel, basis, precision=lax.Precision.HIGHEST, preferred_element_type=jnp.float32
    )
    return product + damping[0] * mean_diagonal * basis_rows


def solution(mesh):
    in_specs = (P("vol", None, "space", None, None), P(), P(), P(), P())
    out_specs = P("vol", None)
    return jax.shard_map(body, mesh=mesh, in_specs=in_specs, out_specs=out_specs, check_vma=False)
```

profile of v0, /device:TPU:0, one launch (start us, length us, event | category | flops | bytes accessed | tf_op | source)
XLA Modules:
  0.0 149.4 jit_solution(2289497347999911215)
XLA Ops:
  6.5 0.0 copy-start
  6.5 0.0 reduce-scatter.2.cloned.1.call-start
  6.5 0.9 slice.10
  7.4 1.3 collective-permute-start
  8.7 1.8 %collective-permute-done = bf16[32,1,8,128]{3,2,1,0:T(8,128)(2,1)S(1)} collective-permute-done((bf16[32,1,8,128]{3,2,1,0:T(8,128)(2,1)S(1)}, bf16[32,1,8,128]{3,2,1,0:T(8,128)(2,1)S(1)}, u32[]{:S(2)}, u32[]{:S(2)}) %collective-permute-start) | collective-permute-done | bytes 65568 | tf_op jit(solution)/shard_map/ppermute | solution.py:10
  10.6 1.1 pad_maximum_fusion
  11.6 1.0 copy.21
  12.6 0.3 pad
  12.9 0.0 copy-start.2
  12.9 0.2 copy.23
  13.2 0.1 slice.11
  13.2 0.0 copy-done
  13.2 0.4 copy-done.2
  13.6 3.9 %fusion.10 = f32[4,8,8,17,32]{4,2,3,1,0:T(8,128)S(1)} fusion(bf16[32,32,3,3,3]{1,0,4,3,2:T(8,128)(2,1)S(1)} %copy-done, bf16[32,6,8,1,7,2]{0,4,5,2,1,3:T(8,128)(2,1)S(1)} %slice.11, bf16[32,6,8,1,8,17]{0,4,5,2,1,3:T(8,128)(2,1)S(1)} %copy.23, pred[8,17]{0,1:T(8,128)(4,1)S(1)} %copy-done.2), kind=kOutput, calls=%fused_computation.12 | convolution fusion | flops 222134272 | bytes 1073288 | tf_op jit(solution)/shard_map/conv_general_dilated | solution.py:27
  17.5 0.4 copy.24
  17.9 0.1 slice.12
  18.0 0.0 copy-start.1
  18.0 0.3 slice.13
  18.4 0.6 copy.30
  19.0 0.0 copy-done.1
  19.0 0.2 fusion.17
  19.2 0.3 copy.27
  19.5 0.2 reshape.21
  19.8 1.7 %convolution_convert_fusion = bf16[864,864]{1,0:T(8,128)(2,1)} fusion(bf16[864,64]{1,0:T(8,128)(2,1)S(1)} %reshape.21), kind=kOutput, calls=%fused_computation.8 | convolution fusion | flops 96297984 | bytes 1603584 | tf_op jit(solution)/shard_map/dot_general | solution.py:37
  21.5 0.0 reduce-scatter.2.cloned.1.call-update
  21.5 30.5 %reduce-scatter.2.cloned.1.call-done = bf16[432,864]{1,0:T(8,128)(2,1)} async-done(((bf16[864,864]{1,0:T(8,128)(2,1)}), bf16[432,864]{1,0:T(8,128)(2,1)}) %reduce-scatter.2.cloned.1.call-update) | async-done | bytes 746512 | tf_op jit(solution)/shard_map/reduce_scatter | solution.py:42
  51.9 74.4 %all-reduce.1 = f32[432,864]{1,0:T(8,128)S(1)} all-reduce(bf16[432,864]{1,0:T(8,128)(2,1)} %reduce-scatter.2.cloned.1.call-done), channel_id=1, replica_groups=mesh['vol'=2,'space'=16] {'space'}, use_global_device_ids=true, to_apply=%region_1.0 | all-reduce | flops 373248 | bytes 2239488 | tf_op jit(solution)/shard_map/psum | solution.py:45
  126.3 0.8 select_reduce_fusion
  127.8 5.5 %psum.15 = f32[]{:T(128)} all-reduce(f32[]{:T(128)} %select_reduce_fusion), channel_id=1, replica_groups=mesh['vol'=2,'space'=16] {'vol'}, use_global_device_ids=true, to_apply=%region_3.4 | all-reduce | flops 1 | bytes 8 | tf_op jit(solution)/shard_map/psum | solution.py:47
  134.0 8.6 %multiply_add_fusion = f32[432,864]{1,0:T(8,128)} fusion(f32[864,864]{1,0:T(8,128)} %param.8, s32[]{:T(128)S(6)} %select_n.9, f32[432,864]{1,0:T(8,128)S(1)} %all-reduce.1, f32[]{:T(128)S(6)} %mul.13), kind=kOutput, calls=%fused_computation.9 | convolution fusion | flops 3870955008 | bytes 7630856 | tf_op jit(solution)/shard_map/dot_general | solution.py:51
  (1 shorter events, 0.0 us)
Async XLA Ops:
  6.5 6.7 %copy-start = (bf16[32,32,3,3,3]{1,0,4,3,2:T(8,128)(2,1)S(1)}, bf16[32,32,3,3,3]{1,0,4,3,2:T(8,128)(2,1)}, u32[]{:S(2)}) copy-start(bf16[32,32,3,3,3]{1,0,4,3,2:T(8,128)(2,1)} %param.6) | copy-start | bytes 165892
  6.5 45.4 %reduce-scatter.2.cloned.1.call-start = ((), (), s32[]{:S(2)}) async-start(), calls=%async_computation.1 | async-start | bytes 2322432 | tf_op jit(solution)/shard_map/reduce_scatter | solution.py:42
  7.4 3.1 %collective-permute-start = (bf16[32,1,8,128]{3,2,1,0:T(8,128)(2,1)S(1)}, bf16[32,1,8,128]{3,2,1,0:T(8,128)(2,1)S(1)}, u32[]{:S(2)}, u32[]{:S(2)}) collective-permute-start(bf16[32,1,8,128]{3,2,1,0:T(8,128)(2,1)S(1)} %slice.10), channel_id=1, source_target_pairs={{1,0},{2,1},{3,2},{4,3},{5,4},{6,5},{7,6},{8,7},{9,8},{10,9},{11,1... | collective-permute-start | bytes 196616 | tf_op jit(solution)/shard_map/ppermute | solution.py:10
  12.9 0.7 copy-start.2
  18.0 1.0 copy-start.1
Sparse Core Ops, SparseCore 0:
  21.6 30.2 reduce-scatter.1
where the time goes:
time: 150 us; the launch traced here: 149 us
  blocking collectives  79.9 us (53%)
  waiting for transfers between devices  32.3 us (22%)
  between operations  14.9 us (10%)
  matrix products  14.1 us (9%)
  local copies, waits for them, and re-layouts  4.89 us (3%)
  other arithmetic  2.03 us (1%)
    psum x1, blocking collectives, body(): row_panel = lax.psum(partial_rows, 'space')  74.4 us
    reduce_scatter x1, waiting for transfers between devices, body(): lax.psum_scatter(local_gram.astype(jnp.bfloat16), 'vol', scatter_dimensio...  30.5 us
    dot_general x1, matrix products, body(): jnp.dot(normed_panel, basis, precision=lax.Precision.HIGHEST, preferred_e...  8.56 us
    psum x1, blocking collectives, body(): trace_value = lax.psum(jnp.trace(diag_block), 'vol')  5.53 us
    conv_general_dilated x1, matrix products, body(): lax.conv_general_dilated(stacked[None], conv_weight, (1, 1, 1), [(0, 0),...  3.85 us
  transfers between devices with their start and end apart: 2, of which 2 were waited for; matrix products, arithmetic and copies ran while one was open for 0% of the time, Pallas kernels for 0%

commit v1 on v0

--- a/solution.py
+++ b/solution.py
@@ -42,7 +42,7 @@
     partial_rows = lax.psum_scatter(
         local_gram.astype(jnp.bfloat16), "vol", scatter_dimension=0, tiled=True
     ).astype(jnp.float32)
-    row_panel = lax.psum(partial_rows, "space")
+    row_panel = jnp.sum(lax.all_gather(partial_rows, "space"), axis=0)
     diag_block = lax.dynamic_slice_in_dim(row_panel, row_start, panel_rows, 1)
     trace_value = lax.psum(jnp.trace(diag_block), "vol")
     normed_panel = row_panel / total_patches

time: 150 us -> 214 us (1.43)
  waiting for transfers between devices: 32.3 us -> 159 us
  blocking collectives: 79.9 us -> 5.53 us
  other arithmetic: 2.03 us -> 13.4 us
    all_gather x0 -> x1, waiting for transfers between devices: none -> 127 us  [body(): row_panel = jnp.sum(lax.all_gather(partial_rows, 'space'), axis=0)]
    psum x1 -> x0, blocking collectives: 74.4 us -> none  [body(): row_panel = lax.psum(partial_rows, 'space')]
    reduce_sum x0 -> x1, other arithmetic: none -> 9.02 us  [body(): row_panel = jnp.sum(lax.all_gather(partial_rows, 'space'), axis=0)]
    all_gather x0 -> x1, other arithmetic: none -> 2.36 us  [body(): row_panel = jnp.sum(lax.all_gather(partial_rows, 'space'), axis=0)]
  transfers between devices with their start and end apart: 2 -> 3, of which waited for: 2 -> 3; matrix products, arithmetic and copies ran while one was open for 0% -> 0% of each run, Pallas kernels for 0% -> 0%
where the time goes in v1:
time: 214 us; the launch traced here: 213 us
  waiting for transfers between devices  159 us (74%)
  between operations  14.9 us (7%)
  matrix products  14.1 us (7%)
  other arithmetic  13.4 us (6%)
  blocking collectives  5.53 us (3%)
  local copies, waits for them, and re-layouts  4.89 us (2%)
    all_gather x1, waiting for transfers between devices, body(): row_panel = jnp.sum(lax.all_gather(partial_rows, 'space'), axis=0)  127 us
    reduce_scatter x1, waiting for transfers between devices, body(): lax.psum_scatter(local_gram.astype(jnp.bfloat16), 'vol', scatter_dimensio...  30.4 us
    reduce_sum x1, other arithmetic, body(): row_panel = jnp.sum(lax.all_gather(partial_rows, 'space'), axis=0)  9.02 us
    dot_general x1, matrix products, body(): jnp.dot(normed_panel, basis, precision=lax.Precision.HIGHEST, preferred_e...  8.56 us
    psum x1, blocking collectives, body(): trace_value = lax.psum(jnp.trace(diag_block), 'vol')  5.53 us
  transfers between devices with their start and end apart: 3, of which 3 were waited for; matrix products, arithmetic and copies ran while one was open for 0% of the time, Pallas kernels for 0%

profile of v1, /device:TPU:0, one launch (start us, length us, event | category | flops | bytes accessed | tf_op | source)
XLA Modules:
  0.0 213.3 jit_solution(3680159464214849132)
XLA Ops:
  6.5 0.0 copy-start
  6.5 0.0 reduce-scatter.2.cloned.1.call-start
  6.5 0.9 slice.10
  7.4 1.3 collective-permute-start
  8.7 1.8 collective-permute-done
  10.6 1.1 pad_maximum_fusion
  11.6 1.0 copy.26
  12.6 0.3 pad
  12.9 0.0 copy-start.2
  12.9 0.2 copy.28
  13.2 0.1 slice.11
  13.2 0.0 copy-done
  13.2 0.4 copy-done.2
  13.6 3.9 %fusion.10 = f32[4,8,8,17,32]{4,2,3,1,0:T(8,128)S(1)} fusion(bf16[32,32,3,3,3]{1,0,4,3,2:T(8,128)(2,1)S(1)} %copy-done, bf16[32,6,8,1,7,2]{0,4,5,2,1,3:T(8,128)(2,1)S(1)} %slice.11, bf16[32,6,8,1,8,17]{0,4,5,2,1,3:T(8,128)(2,1)S(1)} %copy.28, pred[8,17]{0,1:T(8,128)(4,1)S(1)} %copy-done.2), kind=kOutput, calls=%fused_computation.12 | convolution fusion | flops 222134272 | bytes 1073288 | tf_op jit(solution)/shard_map/conv_general_dilated | solution.py:27
  17.5 0.4 copy.29
  17.9 0.1 slice.12
  18.0 0.0 copy-start.1
  18.0 0.3 slice.13
  18.4 0.6 copy.35
  19.0 0.0 copy-done.1
  19.0 0.2 fusion.17
  19.2 0.3 copy.32
  19.5 0.2 reshape.21
  19.8 1.7 convolution_convert_fusion
  21.5 0.0 reduce-scatter.2.cloned.1.call-update
  21.5 0.0 all-gather.3.cloned.1.call-start
  21.5 30.4 %reduce-scatter.2.cloned.1.call-done = bf16[432,864]{1,0:T(8,128)(2,1)} async-done(((bf16[864,864]{1,0:T(8,128)(2,1)}), bf16[432,864]{1,0:T(8,128)(2,1)}) %reduce-scatter.2.cloned.1.call-update) | async-done | bytes 746512 | tf_op jit(solution)/shard_map/reduce_scatter | solution.py:42
  51.9 2.4 %all_gather.12 = f32[432,864]{1,0:T(8,128)} convert(bf16[432,864]{1,0:T(8,128)(2,1)} %reduce-scatter.2.cloned.1.call-done) | non-fusion elementwise | flops 373248 | bytes 2239488 | tf_op jit(solution)/shard_map/all_gather | solution.py:45
  54.3 0.0 all-gather.3.cloned.1.call-update
  54.3 126.9 %all-gather.3.cloned.1.call-done = f32[6912,864]{1,0:T(8,128)} async-done(((f32[432,864]{1,0:T(8,128)}), f32[6912,864]{1,0:T(8,128)}) %all-gather.3.cloned.1.call-update) | async-done | bytes 23887888 | tf_op jit(solution)/shard_map/all_gather | solution.py:45
  181.2 9.0 %reduce_sum.19 = f32[432,864]{1,0:T(8,128)S(1)} reduce(f32[16,432,864]{2,1,0:T(8,128)} %bitcast.24, f32[]{:T(128)} %constant.10.clone.1), dimensions={0}, to_apply=%region_1.0 | reduce | flops 5598720 | bytes 25380868 | tf_op jit(solution)/shard_map/reduce_sum | solution.py:45
  190.3 0.8 select_reduce_fusion
  191.7 5.5 %psum.7 = f32[]{:T(128)} all-reduce(f32[]{:T(128)} %select_reduce_fusion), channel_id=1, replica_groups=mesh['vol'=2,'space'=16] {'vol'}, use_global_device_ids=true, to_apply=%region_3.4 | all-reduce | flops 1 | bytes 8 | tf_op jit(solution)/shard_map/psum | solution.py:47
  197.9 8.6 %multiply_add_fusion = f32[432,864]{1,0:T(8,128)} fusion(f32[864,864]{1,0:T(8,128)} %param.8, s32[]{:T(128)S(6)} %select_n.9, f32[432,864]{1,0:T(8,128)S(1)} %reduce_sum.19, f32[]{:T(128)S(6)} %mul.13), kind=kOutput, calls=%fused_computation.9 | convolution fusion | flops 3870955008 | bytes 7630856 | tf_op jit(solution)/shard_map/dot_general | solution.py:51
  (1 shorter events, 0.0 us)
Async XLA Ops:
  6.5 6.7 %copy-start = (bf16[32,32,3,3,3]{1,0,4,3,2:T(8,128)(2,1)S(1)}, bf16[32,32,3,3,3]{1,0,4,3,2:T(8,128)(2,1)}, u32[]{:S(2)}) copy-start(bf16[32,32,3,3,3]{1,0,4,3,2:T(8,128)(2,1)} %param.6) | copy-start | bytes 165892
  6.5 45.4 %reduce-scatter.2.cloned.1.call-start = ((), (), s32[]{:S(2)}) async-start(), calls=%async_computation.1 | async-start | bytes 2322432 | tf_op jit(solution)/shard_map/reduce_scatter | solution.py:42
  7.4 3.1 %collective-permute-start = (bf16[32,1,8,128]{3,2,1,0:T(8,128)(2,1)S(1)}, bf16[32,1,8,128]{3,2,1,0:T(8,128)(2,1)S(1)}, u32[]{:S(2)}, u32[]{:S(2)}) collective-permute-start(bf16[32,1,8,128]{3,2,1,0:T(8,128)(2,1)S(1)} %slice.10), channel_id=1, source_target_pairs={{1,0},{2,1},{3,2},{4,3},{5,4},{6,5},{7,6},{8,7},{9,8},{10,9},{11,1... | collective-permute-start | bytes 196616 | tf_op jit(solution)/shard_map/ppermute | solution.py:10
  12.9 0.7 copy-start.2
  18.0 1.0 copy-start.1
  21.5 159.7 %all-gather.3.cloned.1.call-start = ((), (), s32[]{:S(2)}) async-start(), calls=%async_computation.2 | async-start | bytes 26320896 | tf_op jit(solution)/shard_map/all_gather | solution.py:45
Sparse Core Ops, SparseCore 0:
  21.6 30.2 reduce-scatter.1
  54.5 126.7 all-gather.2
